TPU v7x, 32 devices: a whole 2x2x4 slice. The times are simulated.
32 devices in a mesh: groups: 2 (over y), bank: 4 (over x, core), tensor: 4 (over z).
Axes of the slice: x: 2, y: 2, z: 4, core: 2. Of those that a mesh axis runs over, the one named last changes fastest.
Arguments:
- normed: bfloat16 [6144, 8192], P(('groups', 'bank'), 'tensor'), parts along dimension 0, may hold values from -6 to 6
- turn_persona_ids: int32 [384], P(('groups', 'bank')), parts along dimension 0, may hold values from 0 to 127, as said below
- persona_bank_row: int32 [256], P('groups'), parts along dimension 0, may hold values from 0 to 127, as said below
- key_weight: bfloat16 [8192, 1024], P('tensor'), may hold values from -0.0625 to 0.0625
- value_weight: bfloat16 [8192, 1024], P('tensor'), may hold values from -0.0625 to 0.0625
- adapter_down_factor: bfloat16 [256, 64, 8192], P(('groups', 'bank'), None, 'tensor'), parts along dimension 0, may hold values from -0.0625 to 0.0625
- adapter_up_factor: bfloat16 [256, 64, 1024], P(('groups', 'bank'), None, 'tensor'), parts along dimension 0, may hold values from -0.375 to 0.375
Outputs:
- keys: bfloat16 [6144, 1024], P(('groups', 'bank'), 'tensor'), parts along dimension 0
- values: bfloat16 [6144, 1024], P(('groups', 'bank'), 'tensor'), parts along dimension 0
There are 2 independent parts, one for each index of `groups`. A program takes and returns all parts, laid end to end along the dimension named above; an argument that names none is the same for every part. Nothing has to cross between parts.
Inputs may be any that keep to these rules, and one draw needn't show every extreme that they name: `turn_persona_ids`: the 48 turns of each bank index use personas whose rows lie on exactly 4 bank indices (row // 32), 12 turns for each of them, naming exactly 2 distinct personas of each. A permutation of the window's personas; row persona_bank_row[w] of adapter_down_factor and adapter_up_factor is persona w's adapter.
All inputs are finite; a program needn't handle non-finite values.
Results may differ from a plain program's by a relative error of at most 0.014.
Values may be sent and summed in bfloat16 or wider, within the bound.
A program may use at most 128 MiB of HBM per device.

v0:
```python
import jax
import jax.numpy as jnp
from jax import lax
from jax.sharding import PartitionSpec as P

CAP = 12


adapter_scale = 2.0


def shards(
    normed,
    turn_persona_ids,
    persona_bank_row,
    key_weight,
    value_weight,
    adapter_down_factor,
    adapter_up_factor,
):
    banks = lax.axis_size("bank")
    local_slots = adapter_down_factor.shape[0]
    width_here = normed.shape[1]
    local_columns = adapter_up_factor.shape[2]
    turn_count = turn_persona_ids.shape[0]
    count_of_tokens = normed.shape[0]
    seg_len = count_of_tokens // turn_count
    window_size = persona_bank_row.shape[0]
    rows_per_turn = normed.reshape(turn_count, seg_len, width_here)
    window_ids = jnp.arange(window_size, dtype=jnp.int32)
    persona_match = turn_persona_ids[:, None] == window_ids[None, :]
    turn_slot = jnp.sum(jnp.where(persona_match, persona_bank_row[None, :], 0), axis=1)
    owner = turn_slot // local_slots
    local = turn_slot % local_slots
    partial_both = jnp.stack(
        [
            jnp.dot(normed, key_weight, preferred_element_type=jnp.float32),
            jnp.dot(normed, value_weight, preferred_element_type=jnp.float32),
        ]
    )
    reduced_sum = lax.psum_scatter(
        partial_both.astype(jnp.bfloat16), "tensor", scatter_dimension=2, tiled=True
    ).astype(jnp.float32)
    turn_ids = jnp.arange(turn_count, dtype=jnp.int32)
    same_owner = owner[:, None] == owner[None, :]
    earlier = turn_ids[:, None] > turn_ids[None, :]
    position = jnp.sum((same_owner & earlier).astype(jnp.int32), axis=1)
    place = owner * CAP + position
    entries = banks * CAP
    entry_ids = jnp.arange(entries, dtype=jnp.int32)
    entry_match = place[None, :] == entry_ids[:, None]
    filled = jnp.any(entry_match, axis=1)
    source = jnp.sum(jnp.where(entry_match, turn_ids[None, :], 0), axis=1)
    send_rows = jnp.where(filled[:, None, None], rows_per_turn[source], jnp.zeros((), jnp.bfloat16))
    send_rows = send_rows.reshape(banks, CAP, seg_len, width_here)
    send_slots = jnp.where(filled, local[source], 0).reshape(banks, CAP)
    received_slots = lax.all_to_all(send_slots, "bank", split_axis=0, concat_axis=0, tiled=True)
    got_rows = lax.all_to_all(send_rows, "bank", split_axis=0, concat_axis=0, tiled=True)

    def project_down(element_entry):
        row_portion, slot_portion = element_entry
        return jnp.einsum(
            "qyn,qxn->qyx",
            row_portion,
            adapter_down_factor[slot_portion],
            preferred_element_type=jnp.float32,
        )

    inner_part = lax.map(project_down, (got_rows, received_slots))
    inner_full = lax.psum(inner_part.astype(jnp.bfloat16), "tensor")
    correction = jnp.einsum(
        "lvdw,lvwe->lvde",
        inner_full,
        adapter_up_factor[received_slots],
        preferred_element_type=jnp.float32,
    )
    returned = lax.all_to_all(
        correction.astype(jnp.bfloat16), "bank", split_axis=0, concat_axis=0, tiled=True
    ).astype(correction.dtype)
    value_update = returned.reshape(entries, seg_len, local_columns)[place]
    keys = reduced_sum[0].astype(jnp.bfloat16)
    values = (
        reduced_sum[1] + adapter_scale * value_update.reshape(count_of_tokens, local_columns)
    ).astype(jnp.bfloat16)
    return (keys, values)


def solution(mesh):
    placed = (
        P(("groups", "bank"), "tensor"),
        P(("groups", "bank")),
        P("groups"),
        P("tensor", None),
        P("tensor", None),
        P(("groups", "bank"), None, "tensor"),
        P(("groups", "bank"), None, "tensor"),
    )
    return jax.shard_map(
        shards,
        mesh=mesh,
        in_specs=placed,
        out_specs=(P(("groups", "bank"), "tensor"), P(("groups", "bank"), "tensor")),
        check_vma=False,
    )
```

profile of v0, /device:TPU:0, one launch (start us, length us, event | category | flops | bytes accessed | tf_op | source)
XLA Modules:
  0.0 208.1 jit_solution(9457709752385211105)
XLA Ops:
  7.2 1.0 select_reduce_fusion.1
  8.7 0.8 gather_fusion.2
  9.4 0.7 select_n.107
  10.1 4.2 %all-to-all-start.1 = ((s32[4,1,12]{2,1,0:T(1,128)}), s32[4,1,12]{2,1,0:T(1,128)S(1)}, u32[]{:S(2)}, u32[]{:S(2)}) async-start(s32[4,1,12]{2,1,0:T(1,128)} %bitcast.12), calls=%async_computation.2 | async-start | bytes 4096 | tf_op jit(solution)/shard_map/all_to_all | solution.py:57
  14.4 2.5 %gather_fusion.1 = bf16[48,16,2048]{2,1,0:T(8,128)(2,1)} fusion(bf16[48,16,2048]{2,1,0:T(8,128)(2,1)S(1)} %bitcast.76, s32[1024]{0:T(1024)S(1)} %pad_clamp_fusion.3), kind=kCustom, calls=%fused_computation.1 | custom fusion | bytes 6291648 | tf_op jit(solution)/shard_map/gather | solution.py:54
  16.9 3.9 %broadcast_select_fusion = bf16[4,12,16,2048]{3,2,1,0:T(8,128)(2,1)} fusion(bf16[4,12,16,2048]{3,2,1,0:T(8,128)(2,1)} %bitcast.77, pred[4,12]{1,0:T(4,128)(4,1)S(1)} %broadcast_in_dim.64), kind=kLoop, calls=%fused_computation.16 | loop fusion | flops 1572864 | bytes 6291504 | tf_op jit(solution)/shard_map/jit(_where)/select_n | solution.py:54
  20.8 4.6 %all-to-all-start = ((bf16[4,12,16,2048]{3,2,1,0:T(8,128)(2,1)}), bf16[4,12,16,2048]{3,2,1,0:T(8,128)(2,1)}, u32[]{:S(2)}, u32[]{:S(2)}) async-start(bf16[4,12,16,2048]{3,2,1,0:T(8,128)(2,1)} %broadcast_select_fusion), calls=%async_computation.1 | async-start | bytes 6291456 | tf_op jit(solution)/shard_map/all_to_all | solution.py:58
  25.5 6.9 %fusion.6 = bf16[1,768,1024]{2,1,0:T(8,128)(2,1)} fusion(bf16[768,2048]{1,0:T(8,128)(2,1)S(1)} %copy-done, bf16[2048,1024]{1,0:T(8,128)(2,1)} %param.12), kind=kOutput, calls=%fused_computation.19 | convolution fusion | flops 3222011904 | bytes 8912896 | tf_op jit(solution)/shard_map/dot_general | solution.py:37
  32.4 4.6 %fusion.7 = bf16[1,768,1024]{2,1,0:T(8,128)(2,1)} fusion(bf16[768,2048]{1,0:T(8,128)(2,1)S(1)} %copy-done, bf16[2048,1024]{1,0:T(8,128)(2,1)S(1)} %copy-done.2), kind=kOutput, calls=%fused_computation.20 | convolution fusion | flops 3222011904 | bytes 8912896 | tf_op jit(solution)/shard_map/dot_general | solution.py:38
  37.0 25.5 %all-to-all-done = bf16[4,12,16,2048]{3,2,1,0:T(8,128)(2,1)} async-done(((bf16[4,12,16,2048]{3,2,1,0:T(8,128)(2,1)}), bf16[4,12,16,2048]{3,2,1,0:T(8,128)(2,1)}, u32[]{:S(2)}, u32[]{:S(2)}) %all-to-all-start) | async-done | bytes 3145760 | tf_op jit(solution)/shard_map/all_to_all | solution.py:58
  62.5 36.2 %while.10 = (s32[]{:T(128)}, bf16[4,12,16,64]{3,2,1,0:T(8,128)(2,1)S(1)}, bf16[4,12,16,2048]{3,2,1,0:T(8,128)(2,1)}, s32[4,12]{1,0:T(4,128)S(1)}, bf16[32,64,2048]{2,1,0:T(8,128)(2,1)}, /*index=5*/s32[]{:T(128)}) while((s32[]{:T(128)}, bf16[4,12,16,64]{3,2,1,0:T(8,128)(2,1)S(1)}, bf16[4,12,16,2048]{3,2,1,0:T(8,128)(2,1)}, ...), condition=%wide.region_6.7_spmd, body=%wide.region_5.6_spmd.sunk | while | flops 50332708 | bytes 10327305 | solution.py:69
  62.5 5.9 %gather_fusion = bf16[12,64,2048]{2,1,0:T(8,128)(2,1)} fusion(bf16[32,64,2048]{2,1,0:T(8,128)(2,1)} %get-tuple-element.89, s32[1024]{0:T(1024)S(1)} %pad_clamp_fusion.5), kind=kCustom, calls=%fused_computation.clone.1 | custom fusion | bytes 6291504 | tf_op jit(solution)/shard_map/while/body/eval_jaxpr/gather | solution.py:65
  68.4 3.1 %fusion.27 = bf16[4,12,16,64]{3,2,1,0:T(8,128)(2,1)S(1)} fusion(bf16[4,12,16,64]{3,2,1,0:T(8,128)(2,1)S(1)} %get-tuple-element.80, s32[]{:T(128)} %get-tuple-element.79, bf16[12,64,2048]{2,1,0:T(8,128)(2,1)} %gather_fusion, bf16[4,12,16,2048]{3,2,1,0:T(8,128)(2,1)} %get-tuple-element.87), kind=kOutput, calls=%fused_computation.6.clone.1 | convolution fusion | flops 50331648 | bytes 4031488 | tf_op jit(solution)/shard_map/while/body/eval_jaxpr/qyn,qxn->qyx/dot_general | solution.py:62
  71.5 5.9 %gather_fusion = bf16[12,64,2048]{2,1,0:T(8,128)(2,1)} fusion(bf16[32,64,2048]{2,1,0:T(8,128)(2,1)} %get-tuple-element.89, s32[1024]{0:T(1024)S(1)} %pad_clamp_fusion.5), kind=kCustom, calls=%fused_computation.clone.1 | custom fusion | bytes 6291504 | tf_op jit(solution)/shard_map/while/body/eval_jaxpr/gather | solution.py:65
  77.4 3.1 %fusion.27 = bf16[4,12,16,64]{3,2,1,0:T(8,128)(2,1)S(1)} fusion(bf16[4,12,16,64]{3,2,1,0:T(8,128)(2,1)S(1)} %get-tuple-element.80, s32[]{:T(128)} %get-tuple-element.79, bf16[12,64,2048]{2,1,0:T(8,128)(2,1)} %gather_fusion, bf16[4,12,16,2048]{3,2,1,0:T(8,128)(2,1)} %get-tuple-element.87), kind=kOutput, calls=%fused_computation.6.clone.1 | convolution fusion | flops 50331648 | bytes 4031488 | tf_op jit(solution)/shard_map/while/body/eval_jaxpr/qyn,qxn->qyx/dot_general | solution.py:62
  80.6 5.9 %gather_fusion = bf16[12,64,2048]{2,1,0:T(8,128)(2,1)} fusion(bf16[32,64,2048]{2,1,0:T(8,128)(2,1)} %get-tuple-element.89, s32[1024]{0:T(1024)S(1)} %pad_clamp_fusion.5), kind=kCustom, calls=%fused_computation.clone.1 | custom fusion | bytes 6291504 | tf_op jit(solution)/shard_map/while/body/eval_jaxpr/gather | solution.py:65
  86.5 3.1 %fusion.27 = bf16[4,12,16,64]{3,2,1,0:T(8,128)(2,1)S(1)} fusion(bf16[4,12,16,64]{3,2,1,0:T(8,128)(2,1)S(1)} %get-tuple-element.80, s32[]{:T(128)} %get-tuple-element.79, bf16[12,64,2048]{2,1,0:T(8,128)(2,1)} %gather_fusion, bf16[4,12,16,2048]{3,2,1,0:T(8,128)(2,1)} %get-tuple-element.87), kind=kOutput, calls=%fused_computation.6.clone.1 | convolution fusion | flops 50331648 | bytes 4031488 | tf_op jit(solution)/shard_map/while/body/eval_jaxpr/qyn,qxn->qyx/dot_general | solution.py:62
  89.6 5.9 %gather_fusion = bf16[12,64,2048]{2,1,0:T(8,128)(2,1)} fusion(bf16[32,64,2048]{2,1,0:T(8,128)(2,1)} %get-tuple-element.89, s32[1024]{0:T(1024)S(1)} %pad_clamp_fusion.5), kind=kCustom, calls=%fused_computation.clone.1 | custom fusion | bytes 6291504 | tf_op jit(solution)/shard_map/while/body/eval_jaxpr/gather | solution.py:65
  95.5 3.1 %fusion.27 = bf16[4,12,16,64]{3,2,1,0:T(8,128)(2,1)S(1)} fusion(bf16[4,12,16,64]{3,2,1,0:T(8,128)(2,1)S(1)} %get-tuple-element.80, s32[]{:T(128)} %get-tuple-element.79, bf16[12,64,2048]{2,1,0:T(8,128)(2,1)} %gather_fusion, bf16[4,12,16,2048]{3,2,1,0:T(8,128)(2,1)} %get-tuple-element.87), kind=kOutput, calls=%fused_computation.6.clone.1 | convolution fusion | flops 50331648 | bytes 4031488 | tf_op jit(solution)/shard_map/while/body/eval_jaxpr/qyn,qxn->qyx/dot_general | solution.py:62
  98.6 0.7 copy-done.1
  99.4 3.8 %pad_maximum_fusion = bf16[2,768,1024]{2,1,0:T(8,128)(2,1)} fusion(bf16[1,768,1024]{2,1,0:T(8,128)(2,1)} %fusion.7, bf16[1,768,1024]{2,1,0:T(8,128)(2,1)} %fusion.6), kind=kLoop, calls=%fused_computation.15 | loop fusion | flops 1572864 | bytes 6291456 | tf_op jit(solution)/shard_map/stack | solution.py:35
  103.3 3.1 %gather_fusion.3 = bf16[48,64,256]{2,1,0:T(8,128)(2,1)} fusion(bf16[32,64,256]{2,1,0:T(8,128)(2,1)} %param.15, s32[1024]{0:T(1024)S(1)} %pad_clamp_fusion.2), kind=kCustom, calls=%fused_computation.3 | custom fusion | bytes 3145920 | tf_op jit(solution)/shard_map/gather | solution.py:74
  106.4 28.7 %all-reduce.2.cloned.1.call-done = bf16[4,12,16,64]{3,2,1,0:T(8,128)(2,1)} async-done(((bf16[4,12,16,64]{3,2,1,0:T(8,128)(2,1)}), bf16[4,12,16,64]{3,2,1,0:T(8,128)(2,1)}) %all-reduce.2.cloned.1.call-update) | async-done | bytes 98320 | tf_op jit(solution)/shard_map/psum | solution.py:70
  135.1 2.6 %convolution_convert_fusion.2 = bf16[4,12,16,256]{3,2,1,0:T(8,128)(2,1)} fusion(bf16[4,12,16,64]{3,2,1,0:T(8,128)(2,1)} %all-reduce.2.cloned.1.call-done, bf16[4,12,64,256]{3,2,1,0:T(8,128)(2,1)} %bitcast.78), kind=kOutput, calls=%fused_computation.21 | convolution fusion | flops 25362432 | bytes 2064384 | tf_op jit(solution)/shard_map/lvdw,lvwe->lvde/dot_general | solution.py:71
  137.7 3.5 %all-to-all-start.2 = ((bf16[4,12,16,256]{3,2,1,0:T(8,128)(2,1)}), bf16[4,12,16,256]{3,2,1,0:T(8,128)(2,1)S(1)}, u32[]{:S(2)}, u32[]{:S(2)}) async-start(bf16[4,12,16,256]{3,2,1,0:T(8,128)(2,1)} %convolution_convert_fusion.2), calls=%async_computation.3 | async-start | bytes 786432 | tf_op jit(solution)/shard_map/all_to_all | solution.py:77
  141.2 7.4 %all-to-all-done.2 = bf16[4,12,16,256]{3,2,1,0:T(8,128)(2,1)S(1)} async-done(((bf16[4,12,16,256]{3,2,1,0:T(8,128)(2,1)}), bf16[4,12,16,256]{3,2,1,0:T(8,128)(2,1)S(1)}, u32[]{:S(2)}, u32[]{:S(2)}) %all-to-all-start.2) | async-done | bytes 393248 | tf_op jit(solution)/shard_map/all_to_all | solution.py:77
  148.6 1.0 bitcast_convert_fusion
  149.6 2.6 %gather_fusion.4 = f32[48,16,256]{2,1,0:T(8,128)} fusion(f32[48,16,256]{2,1,0:T(8,128)} %bitcast_convert_fusion, s32[1024]{0:T(1024)S(1)} %pad_clamp_fusion.1), kind=kCustom, calls=%fused_computation.4 | custom fusion | bytes 1573056 | tf_op jit(solution)/shard_map/gather | solution.py:80
  152.2 2.1 broadcast_multiply_fusion
  154.2 43.2 %reduce-scatter.2.cloned.1.call-done = bf16[2,768,256]{2,1,0:T(8,128)(2,1)} async-done(((bf16[2,768,1024]{2,1,0:T(8,128)(2,1)}), bf16[2,768,256]{2,1,0:T(8,128)(2,1)}) %reduce-scatter.2.cloned.1.call-update) | async-done | bytes 786448 | tf_op jit(solution)/shard_map/reduce_scatter | solution.py:41
  197.5 1.8 slice_bitcast_fusion.1
  199.2 2.1 fusion.8
  (33 shorter events, 0.9 us)
Async XLA Ops:
  7.2 7.2 %copy-start = (bf16[768,2048]{1,0:T(8,128)(2,1)S(1)}, bf16[768,2048]{1,0:T(8,128)(2,1)}, u32[]{:S(2)}) copy-start(bf16[768,2048]{1,0:T(8,128)(2,1)} %param.9) | copy-start | bytes 9437188
  10.1 10.7 %all-to-all-start.1 = ((s32[4,1,12]{2,1,0:T(1,128)}), s32[4,1,12]{2,1,0:T(1,128)S(1)}, u32[]{:S(2)}, u32[]{:S(2)}) async-start(s32[4,1,12]{2,1,0:T(1,128)} %bitcast.12), calls=%async_computation.2 | async-start | bytes 4096 | tf_op jit(solution)/shard_map/all_to_all | solution.py:57
  20.8 41.7 %all-to-all-start = ((bf16[4,12,16,2048]{3,2,1,0:T(8,128)(2,1)}), bf16[4,12,16,2048]{3,2,1,0:T(8,128)(2,1)}, u32[]{:S(2)}, u32[]{:S(2)}) async-start(bf16[4,12,16,2048]{3,2,1,0:T(8,128)(2,1)} %broadcast_select_fusion), calls=%async_computation.1 | async-start | bytes 6291456 | tf_op jit(solution)/shard_map/all_to_all | solution.py:58
  25.4 109.6 %all-reduce.2.cloned.1.call-start = ((), (), s32[]{:S(2)}) async-start(), calls=%async_computation.5 | async-start | bytes 393216 | tf_op jit(solution)/shard_map/psum | solution.py:70
  25.5 6.9 %copy-start.2 = (bf16[2048,1024]{1,0:T(8,128)(2,1)S(1)}, bf16[2048,1024]{1,0:T(8,128)(2,1)}, u32[]{:S(2)}) copy-start(bf16[2048,1024]{1,0:T(8,128)(2,1)} %param.13) | copy-start | bytes 12582916
  98.6 0.7 copy-start.1
  99.3 98.2 %reduce-scatter.2.cloned.1.call-start = ((), (), s32[]{:S(2)}) async-start(), calls=%async_computation.4 | async-start | bytes 3932160 | tf_op jit(solution)/shard_map/reduce_scatter | solution.py:41
  137.7 10.9 %all-to-all-start.2 = ((bf16[4,12,16,256]{3,2,1,0:T(8,128)(2,1)}), bf16[4,12,16,256]{3,2,1,0:T(8,128)(2,1)S(1)}, u32[]{:S(2)}, u32[]{:S(2)}) async-start(bf16[4,12,16,256]{3,2,1,0:T(8,128)(2,1)} %convolution_convert_fusion.2), calls=%async_computation.3 | async-start | bytes 786432 | tf_op jit(solution)/shard_map/all_to_all | solution.py:77
Sparse Core Ops, SparseCore 0:
  99.5 35.5 all-reduce.1
  137.5 59.9 reduce-scatter.1
where the time goes:
time: 209 us; the launch traced here: 208 us
  waiting for transfers between devices  105 us (50%)
  local copies, waits for them, and re-layouts  36 us (17%)
  matrix products  26.4 us (13%)
  other arithmetic  14.4 us (7%)
  between operations  14.2 us (7%)
  starting transfers between devices  12.4 us (6%)
    reduce_scatter x1, waiting for transfers between devices, shards(): lax.psum_scatter(partial_both.astype(jnp.bfloat16), 'tensor', scatter_dim...  43.2 us
    psum x1, waiting for transfers between devices, shards(): inner_full = lax.psum(inner_part.astype(jnp.bfloat16), 'tensor')  28.7 us
    all_to_all x1, waiting for transfers between devices, shards(): lax.all_to_all(send_rows, 'bank', split_axis=0, concat_axis=0, tiled=True)  25.5 us
    gather x4, local copies, waits for them, and re-layouts, project_down(): adapter_down_factor[slot_portion]  23.7 us
    dot_general x4, matrix products, project_down(): jnp.einsum('qyn,qxn->qyx', row_portion, adapter_down_factor[slot_portion]...  12.3 us
    all_to_all x1, waiting for transfers between devices, shards(): lax.all_to_all(correction.astype(jnp.bfloat16), 'bank', split_axis=0, con...  7.37 us
    dot_general x1, matrix products, shards(): jnp.dot(normed, key_weight, preferred_element_type=jnp.float32)  6.92 us
    all_to_all x1, starting transfers between devices, shards(): lax.all_to_all(send_rows, 'bank', split_axis=0, concat_axis=0, tiled=True)  4.64 us
  transfers between devices with their start and end apart: 5, of which 4 were waited for; matrix products, arithmetic and copies ran while one was open for 16% of the time, Pallas kernels for 0%

commit v1 on v0

v1 whole, which is shorter than its diff:
```python
import functools

import jax
import jax.numpy as jnp
from jax import lax
from jax.experimental import pallas as pl
from jax.experimental.pallas import tpu as pltpu
from jax.sharding import PartitionSpec as P

ADAPTER_SCALE = 2.0
LANES = 128
BF16 = jnp.bfloat16
F32 = jnp.float32


def kernel(
    n_t,
    n_b,
    step,
    ids,
    table,
    normed_h,
    kw_h,
    vw_h,
    down_h,
    up_h,
    keys_o,
    vals_o,
    x,
    w,
    down,
    up,
    part,
    rcv,
    gbuf,
    gs,
    pts,
    asend,
    arecv,
    big,
    dup,
    own,
    rin,
    sin,
    e,
    delta,
    acc,
    xsem,
    wsem,
    dsem,
    gsem,
    ids_s,
    ids_r,
    ad_s,
    ad_r,
    ssem,
    rsem,
    in_s,
    in_r,
):
    i = lax.axis_index("tensor")
    me = lax.axis_index("bank")
    tokens, feats = x.shape
    slots, rank, _ = down.shape
    cols = up.shape[2]
    turns = ids.shape[0]
    seg = tokens // turns
    chunks = tokens // step
    pair = 2 * rank
    half = tokens // 2
    blocks = n_b * pair // LANES

    def rows_of(c):
        return pl.ds(pl.multiple_of(c * step, step), step)

    def w_copies(d):
        at = pl.ds(pl.multiple_of(d * cols, cols), cols)
        return (
            pltpu.make_async_copy(kw_h.at[:, at], w.at[d, :, pl.ds(0, cols)], wsem.at[d, 0]),
            pltpu.make_async_copy(vw_h.at[:, at], w.at[d, :, pl.ds(cols, cols)], wsem.at[d, 1]),
        )

    def x_copy(c):
        return pltpu.make_async_copy(normed_h.at[rows_of(c)], x.at[rows_of(c)], xsem.at[c])

    down_copy = pltpu.make_async_copy(down_h, down, dsem.at[0])
    up_copy = pltpu.make_async_copy(up_h, up, dsem.at[1])

    def dest(s):
        k = n_t - 1 - s // 2
        return i + k * (1 - 2 * lax.rem(s, 2))

    def load_w(s, _):
        d = dest(s)

        @pl.when((d >= 0) & (d < n_t))
        def _():
            for copy in w_copies(d):
                copy.start()

        return 0

    x_copy(0).start()
    lax.fori_loop(0, 2, load_w, 0)
    for c in range(1, chunks):
        x_copy(c).start()
    down_copy.start()
    up_copy.start()
    lax.fori_loop(2, 2 * n_t - 1, load_w, 0)

    barrier = pltpu.get_barrier_semaphore()

    def greet(k, _):
        pl.semaphore_signal(barrier, inc=1, device_id={"bank": lax.rem(me + k, n_b)})
        return 0

    lax.fori_loop(1, n_b, greet, 0)

    @pl.when(i > 0)
    def _():
        pl.semaphore_signal(barrier, inc=1, device_id={"tensor": i - 1})

    @pl.when(i < n_t - 1)
    def _():
        pl.semaphore_signal(barrier, inc=1, device_id={"tensor": i + 1})

    lane8 = lax.broadcasted_iota(jnp.int32, (8, LANES), 1)
    row8 = lax.broadcasted_iota(jnp.int32, (8, LANES), 0)

    def scan_turn(t, carry):
        low, high = carry
        slot = table[ids[t]]
        owner = slot // slots
        local = slot - owner * slots
        pts[t] = slot
        here = lane8 == owner
        low = jnp.where(here, jnp.minimum(low, local), low)
        high = jnp.where(here, jnp.maximum(high, local), high)
        return low, high

    low, high = lax.fori_loop(
        0,
        turns,
        scan_turn,
        (jnp.full((8, LANES), slots - 1, jnp.int32), jnp.zeros((8, LANES), jnp.int32)),
    )
    gbuf[me] = jnp.where(row8 == 0, low, high)

    neighbours = (n_b - 1) + (i > 0).astype(jnp.int32) + (i < n_t - 1).astype(jnp.int32)
    pl.semaphore_wait(barrier, neighbours)

    def ids_msg(d, slot):
        return pltpu.make_async_remote_copy(
            src_ref=gbuf.at[me],
            dst_ref=gbuf.at[slot],
            send_sem=ids_s.at[d],
            recv_sem=ids_r.at[slot],
            device_id={"bank": d},
        )

    def send_ids(k, _):
        ids_msg(lax.rem(me + k, n_b), me).start()
        return 0

    lax.fori_loop(1, n_b, send_ids, 0)

    def msg(d, c):
        left = (d < i).astype(jnp.int32)
        return pltpu.make_async_remote_copy(
            src_ref=part.at[d, rows_of(c)],
            dst_ref=rcv.at[left, d, rows_of(c)],
            send_sem=ssem.at[d, c],
            recv_sem=rsem.at[left, d, c],
            device_id={"tensor": i + 1 - 2 * left},
        )

    def arrival(left, d, c):
        return pltpu.make_async_remote_copy(
            src_ref=part.at[d, rows_of(c)],
            dst_ref=rcv.at[left, d, rows_of(c)],
            send_sem=ssem.at[d, c],
            recv_sem=rsem.at[left, d, c],
            device_id={"tensor": (i + 1) - 2 * (i > 0).astype(jnp.int32)},
        )

    at_end = (i == 0) | (i == n_t - 1)

    def project(s, _):
        d = dest(s)

        @pl.when((d >= 0) & (d < n_t))
        def _():
            for copy in w_copies(d):
                copy.wait()

            def chunk(c, _):
                @pl.when(waits_x(s))
                def _():
                    x_copy(c).wait()

                part[d, rows_of(c)] = jnp.dot(
                    x[rows_of(c), :], w[d], preferred_element_type=F32
                ).astype(BF16)

                @pl.when(at_end & (s < 2 * n_t - 4))
                def _():
                    msg(d, c).start()

                return 0

            lax.fori_loop(0, chunks, chunk, 0)

        return 0

    first = 2 * (n_t - 1 - jnp.maximum(i, n_t - 1 - i)) + (i > n_t - 1 - i).astype(jnp.int32)

    def waits_x(s):
        return s == first

    lax.fori_loop(0, 2, project, 0)

    def ids_in(k, _):
        ids_msg(lax.rem(me + k, n_b), lax.rem(me + k, n_b)).wait_recv()
        return 0

    lax.fori_loop(1, n_b, ids_in, 0)
    to_smem = pltpu.make_async_copy(gbuf, gs, gsem.at[0])
    to_smem.start()
    to_smem.wait()
    down_copy.wait()
    up_copy.wait()

    def bank_rows(d):
        return pl.ds(pl.multiple_of(d * pair, pair), pair)

    def fill(d, to):
        for j in range(2):
            slot = gs[d, j, me]
            at = pl.ds(pl.multiple_of(d * pair + j * rank, rank), rank)
            to[at, pl.ds(0, feats)] = down[slot]
            to[at, pl.ds(feats, cols)] = up[slot]

    def adapter_msg(d, slot):
        return pltpu.make_async_remote_copy(
            src_ref=asend.at[bank_rows(d)],
            dst_ref=arecv.at[bank_rows(slot)],
            send_sem=ad_s.at[d],
            recv_sem=ad_r.at[slot],
            device_id={"bank": d},
        )

    def send_adapter(k, _):
        d = lax.rem(me + k, n_b)
        fill(d, asend)
        adapter_msg(d, me).start()
        return 0

    lax.fori_loop(1, n_b, send_adapter, 0)
    fill(me, arecv)

    lax.fori_loop(2, 2 * n_t - 1, project, 0)

    def relay(d, left):
        def chunk(c, _):
            arrival(left, d, c).wait_recv()
            part[d, rows_of(c)] = (
                part[d, rows_of(c)].astype(F32) + rcv[left, d, rows_of(c)].astype(F32)
            ).astype(BF16)
            msg(d, c).start()
            return 0

        return chunk

    def own_start(d):
        def chunk(c, _):
            msg(d, c).start()
            return 0

        return chunk

    def relays(j, _):
        def chunk(c, _):
            right = n_t - 1 - j

            @pl.when((right > i) & (i > 0))
            def _():
                relay(right, 0)(c, 0)

            @pl.when((j < i) & (i < n_t - 1))
            def _():
                relay(j, 1)(c, 0)

            return 0

        return lax.fori_loop(0, chunks, chunk, 0)

    @pl.when((i > 0) & (i < n_t - 1))
    def _():
        lax.fori_loop(0, n_t - 1, relays, 0)

    def adapters_in(k, _):
        d = lax.rem(me + k, n_b)
        adapter_msg(d, d).wait_recv()
        return 0

    lax.fori_loop(1, n_b, adapters_in, 0)
    lane = lax.broadcasted_iota(jnp.int32, (seg, LANES), 1)
    turn_lane = lane // rank

    def choose(t, _):
        slot = pts[t]
        owner = slot // slots
        local = slot - owner * slots
        pts[t] = owner * 2 + (local != gs[me, 0, owner]).astype(jnp.int32)
        return 0

    lax.fori_loop(0, turns, choose, 0)

    def rank_chunk(c, _):
        big[...] = lax.dot_general(
            x[rows_of(c), :],
            arecv[:, :feats],
            (((1,), (1,)), ((), ())),
            preferred_element_type=F32,
        )

        def pick(t, _):
            p = pts[c * (step // seg) + t]
            at = pl.ds(pl.multiple_of(t * seg, seg), seg)
            total = jnp.zeros((seg, LANES), F32)
            for b in range(blocks):
                total = total + jnp.where(
                    turn_lane + 2 * b == p, big[at, b * LANES : (b + 1) * LANES], 0.0
                )
            total = total + pltpu.roll(total, rank, 1)
            dup[pl.ds(pl.multiple_of(c * step + t * seg, seg), seg), :] = total
            return 0

        return lax.fori_loop(0, step // seg, pick, 0)

    lax.fori_loop(0, chunks, rank_chunk, 0)
    low_lane = lax.broadcasted_iota(jnp.int32, (half, LANES), 1) < rank
    own[...] = jnp.where(low_lane, dup[pl.ds(0, half), :], dup[pl.ds(half, half), :])

    def inner_msg(left):
        return pltpu.make_async_remote_copy(
            src_ref=sin.at[left],
            dst_ref=rin.at[left],
            send_sem=in_s.at[left],
            recv_sem=in_r.at[left],
            device_id={"tensor": i + 1 - 2 * left},
        )

    def inner_in(left):
        return pltpu.make_async_remote_copy(
            src_ref=sin.at[left],
            dst_ref=rin.at[left],
            send_sem=in_s.at[left],
            recv_sem=in_r.at[left],
            device_id={"tensor": (i + 1) - 2 * (i > 0).astype(jnp.int32)},
        )

    @pl.when(i == 0)
    def _():
        sin[0] = own[...].astype(BF16)
        inner_msg(0).start()

    @pl.when(i == n_t - 1)
    def _():
        sin[1] = own[...].astype(BF16)
        inner_msg(1).start()

    @pl.when(i == 0)
    def _():
        lax.fori_loop(0, chunks, own_start(1), 0)

    @pl.when(i == n_t - 1)
    def _():
        lax.fori_loop(0, chunks, own_start(n_t - 2), 0)

    dup[pl.ds(0, half), :] = own[...]

    @pl.when(i > 0)
    def _():
        inner_in(0).wait_recv()
        before = rin[0].astype(F32)
        dup[pl.ds(0, half), :] += before

        @pl.when(i < n_t - 1)
        def _():
            sin[0] = (own[...] + before).astype(BF16)
            inner_msg(0).start()

    @pl.when(i < n_t - 1)
    def _():
        inner_in(1).wait_recv()
        after = rin[1].astype(F32)
        dup[pl.ds(0, half), :] += after

        @pl.when(i > 0)
        def _():
            sin[1] = (own[...] + after).astype(BF16)
            inner_msg(1).start()

    total = dup[pl.ds(0, half), :].astype(BF16).astype(F32)
    turned = pltpu.roll(total, rank, 1)
    dup[pl.ds(0, half), :] = jnp.where(low_lane, total, turned)
    dup[pl.ds(half, half), :] = jnp.where(low_lane, turned, total)

    def spread(t, _):
        p = pts[t]
        at = pl.ds(pl.multiple_of(t * seg, seg), seg)
        mine = dup[at, :]
        for b in range(blocks):
            e[at, b * LANES : (b + 1) * LANES] = jnp.where(turn_lane + 2 * b == p, mine, 0.0).astype(
                BF16
            )
        return 0

    lax.fori_loop(0, turns, spread, 0)

    def raise_chunk(c, _):
        delta[rows_of(c), :] = jnp.dot(
            e[rows_of(c), :], arecv[:, feats:], preferred_element_type=F32
        )
        return 0

    lax.fori_loop(0, chunks, raise_chunk, 0)

    def finish(c, _):
        acc[...] = part[i, rows_of(c)].astype(F32)

        @pl.when(i > 0)
        def _():
            arrival(0, i, c).wait_recv()
            acc[...] += rcv[0, i, rows_of(c)].astype(F32)

        @pl.when(i < n_t - 1)
        def _():
            arrival(1, i, c).wait_recv()
            acc[...] += rcv[1, i, rows_of(c)].astype(F32)

        keys_o[rows_of(c), :] = acc[:, :cols].astype(BF16)
        vals_o[rows_of(c), :] = (acc[:, cols:] + ADAPTER_SCALE * delta[rows_of(c), :]).astype(BF16)
        return 0

    lax.fori_loop(0, chunks, finish, 0)

    def sent(d, _):
        @pl.when(d != i)
        def _():
            def chunk(c, _):
                msg(d, c).wait_send()
                return 0

            lax.fori_loop(0, chunks, chunk, 0)

        return 0

    lax.fori_loop(0, n_t, sent, 0)

    def bank_sent(k, _):
        d = lax.rem(me + k, n_b)
        ids_msg(d, me).wait_send()
        adapter_msg(d, me).wait_send()
        return 0

    lax.fori_loop(1, n_b, bank_sent, 0)

    @pl.when(i < n_t - 1)
    def _():
        inner_msg(0).wait_send()

    @pl.when(i > 0)
    def _():
        inner_msg(1).wait_send()


def shards(
    n_t,
    n_b,
    normed,
    turn_persona_ids,
    persona_bank_row,
    key_weight,
    value_weight,
    adapter_down_factor,
    adapter_up_factor,
):
    tokens, feats = normed.shape
    slots, rank, cols = adapter_up_factor.shape
    turns = turn_persona_ids.shape[0]
    step = 256
    chunks = tokens // step
    dma = pltpu.SemaphoreType.DMA
    any_space = pl.BlockSpec(memory_space=pl.ANY)
    smem = pl.BlockSpec(memory_space=pltpu.SMEM)
    vmem = pl.BlockSpec(memory_space=pltpu.VMEM)
    out = jax.ShapeDtypeStruct((tokens, cols), BF16)
    return pl.pallas_call(
        functools.partial(kernel, n_t, n_b, step),
        out_shape=(out, out),
        in_specs=[smem, smem] + [any_space] * 5,
        out_specs=(vmem, vmem),
        scratch_shapes=[
            pltpu.VMEM((tokens, feats), BF16),
            pltpu.VMEM((n_t, feats, 2 * cols), BF16),
            pltpu.VMEM((slots, rank, feats), BF16),
            pltpu.VMEM((slots, rank, cols), BF16),
            pltpu.VMEM((n_t, tokens, 2 * cols), BF16),
            pltpu.VMEM((2, n_t, tokens, 2 * cols), BF16),
            pltpu.VMEM((n_b, 8, LANES), jnp.int32),
            pltpu.SMEM((n_b, 8, LANES), jnp.int32),
            pltpu.SMEM((turns,), jnp.int32),
            pltpu.VMEM((n_b * 2 * rank, feats + cols), BF16),
            pltpu.VMEM((n_b * 2 * rank, feats + cols), BF16),
            pltpu.VMEM((step, n_b * 2 * rank), F32),
            pltpu.VMEM((tokens, LANES), F32),
            pltpu.VMEM((tokens // 2, LANES), F32),
            pltpu.VMEM((2, tokens // 2, LANES), BF16),
            pltpu.VMEM((2, tokens // 2, LANES), BF16),
            pltpu.VMEM((tokens, n_b * 2 * rank), BF16),
            pltpu.VMEM((tokens, cols), F32),
            pltpu.VMEM((step, 2 * cols), F32),
            dma((chunks,)),
            dma((n_t, 2)),
            dma((2,)),
            dma((1,)),
            dma((n_b,)),
            dma((n_b,)),
            dma((n_b,)),
            dma((n_b,)),
            dma((n_t, chunks)),
            dma((2, n_t, chunks)),
            dma((2,)),
            dma((2,)),
        ],
        compiler_params=pltpu.CompilerParams(
            collective_id=0, has_side_effects=True, vmem_limit_bytes=58 * 1024 * 1024
        ),
        cost_estimate=pl.CostEstimate(
            flops=4 * tokens * feats * cols * n_t,
            bytes_accessed=2 * (tokens * feats + 2 * feats * cols * n_t + slots * rank * feats),
            transcendentals=0,
        ),
    )(
        turn_persona_ids,
        persona_bank_row,
        normed,
        key_weight,
        value_weight,
        adapter_down_factor,
        adapter_up_factor,
    )


def solution(mesh):
    placed = (
        P(("groups", "bank"), "tensor"),
        P(("groups", "bank")),
        P("groups"),
        P("tensor", None),
        P("tensor", None),
        P(("groups", "bank"), None, "tensor"),
        P(("groups", "bank"), None, "tensor"),
    )
    return jax.shard_map(
        functools.partial(shards, mesh.shape["tensor"], mesh.shape["bank"]),
        mesh=mesh,
        in_specs=placed,
        out_specs=(P(("groups", "bank"), "tensor"), P(("groups", "bank"), "tensor")),
        check_vma=False,
    )
```

time: 209 us -> 88.2 us (0.42)
  waiting for transfers between devices: 105 us -> 0 us
  Pallas kernels: 0 us -> 83.8 us
  local copies, waits for them, and re-layouts: 36 us -> 3.53 us
  matrix products: 26.4 us -> 0 us
  other arithmetic: 14.4 us -> 0 us
  between operations: 14.2 us -> 0.64 us
  starting transfers between devices: 12.4 us -> 0 us
    pallas_call x0 -> x1, Pallas kernels: none -> 83.8 us  [shards(): pl.pallas_call(functools.partial(kernel, n_t, n_b, step), out_shape=(out,...]
    reduce_scatter x1 -> x0, waiting for transfers between devices: 43.2 us -> none  [shards(): lax.psum_scatter(partial_both.astype(jnp.bfloat16), 'tensor', scatter_dim...]
    all_to_all x3 -> x0, waiting for transfers between devices: 32.8 us -> none  [the longest x1 25.5 us: shards(): lax.all_to_all(send_rows, 'bank', split_axis=0, concat_axis=0, tiled=True)]
    gather x8 -> x0, local copies, waits for them, and re-layouts: 32.7 us -> none  [the longest x4 23.7 us: project_down(): adapter_down_factor[slot_portion]]
    psum x1 -> x0, waiting for transfers between devices: 28.7 us -> none  [shards(): inner_full = lax.psum(inner_part.astype(jnp.bfloat16), 'tensor')]
    dot_general x7 -> x0, matrix products: 26.4 us -> none  [the longest x4 12.3 us: project_down(): jnp.einsum('qyn,qxn->qyx', row_portion, adapter_down_factor[slot_portion]...]
    all_to_all x3 -> x0, starting transfers between devices: 12.3 us -> none  [the longest x1 4.64 us: shards(): lax.all_to_all(send_rows, 'bank', split_axis=0, concat_axis=0, tiled=True)]
    select_n x10 -> x0, other arithmetic: 3.96 us -> none  [the longest x1 3.87 us: shards(): jnp.where(filled[:, None, None], rows_per_turn[source], jnp.zeros((), jnp...]
  transfers between devices with their start and end apart: 5 -> 0, of which waited for: 4 -> 0; matrix products, arithmetic and copies ran while one was open for 16% -> 0% of each run, Pallas kernels for 0% -> 0%
where the time goes in v1:
time: 88.2 us; the launch traced here: 88 us
  Pallas kernels  83.8 us (95%)
  local copies, waits for them, and re-layouts  3.53 us (4%)
    pallas_call x1, Pallas kernels, shards(): pl.pallas_call(functools.partial(kernel, n_t, n_b, step), out_shape=(out,...  83.8 us
    unnamed x2, local copies, waits for them, and re-layouts  3.53 us

profile of v1, /device:TPU:0, one launch (start us, length us, event | category | flops | bytes accessed | tf_op | source)
XLA Modules:
  0.0 88.0 jit_solution(15845894759136105868)
XLA Ops:
  0.6 83.8 %shard_map.86 = (bf16[768,256]{1,0:T(8,128)(2,1)}, bf16[768,256]{1,0:T(8,128)(2,1)}) custom-call(s32[48]{0:T(128)} %ids.1, s32[128]{0:T(128)} %table.1, bf16[768,2048]{1,0:T(8,128)(2,1)} %normed_h.1, bf16[2048,1024]{1,0:T(8,128)(2,1)} %kw_h.1, bf16[2048,1024]{1,0:T(8,128)(2,1)} %vw_h.1, bf16[32,64,2048]{2,1,0:T(8,128)(2,1)} %down_h.1, bf16[32,64,256]{2,1,0:T(8,128)(2,1)} %up_h.1), custom_call_target="tpu_custom_call" | custom-call | flops 6442450944 | bytes 19922944 | tf_op jit(solution)/shard_map/pallas_call | solution.py:500
  84.4 1.8 %copy.11 = bf16[768,256]{1,0:T(8,128)(2,1)} copy(bf16[768,256]{1,0:T(8,128)(2,1)} %get-tuple-element.4) | data formatting | bytes 786432
  86.2 1.8 %copy.12 = bf16[768,256]{1,0:T(8,128)(2,1)} copy(bf16[768,256]{1,0:T(8,128)(2,1)} %get-tuple-element.5) | data formatting | bytes 786432

commit v2 on v1

--- a/solution.py
+++ b/solution.py
@@ -100,29 +100,27 @@
 
         return 0
 
+    barrier = pltpu.get_barrier_semaphore()
+
+    def greet(k, _):
+        pl.semaphore_signal(barrier, inc=1, device_id={"bank": lax.rem(me + k, n_b)})
+        return 0
+
+    lax.fori_loop(1, n_b, greet, 0)
+
+    @pl.when(i > 0)
+    def _():
+        pl.semaphore_signal(barrier, inc=1, device_id={"tensor": i - 1})
+
+    @pl.when(i < n_t - 1)
+    def _():
+        pl.semaphore_signal(barrier, inc=1, device_id={"tensor": i + 1})
+
+    first = 2 * (n_t - 1 - jnp.maximum(i, n_t - 1 - i)) + (i > n_t - 1 - i).astype(jnp.int32)
     x_copy(0).start()
-    lax.fori_loop(0, 2, load_w, 0)
+    load_w(first, 0)
     for c in range(1, chunks):
         x_copy(c).start()
-    down_copy.start()
-    up_copy.start()
-    lax.fori_loop(2, 2 * n_t - 1, load_w, 0)
-
-    barrier = pltpu.get_barrier_semaphore()
-
-    def greet(k, _):
-        pl.semaphore_signal(barrier, inc=1, device_id={"bank": lax.rem(me + k, n_b)})
-        return 0
-
-    lax.fori_loop(1, n_b, greet, 0)
-
-    @pl.when(i > 0)
-    def _():
-        pl.semaphore_signal(barrier, inc=1, device_id={"tensor": i - 1})
-
-    @pl.when(i < n_t - 1)
-    def _():
-        pl.semaphore_signal(barrier, inc=1, device_id={"tensor": i + 1})
 
     lane8 = lax.broadcasted_iota(jnp.int32, (8, LANES), 1)
     row8 = lax.broadcasted_iota(jnp.int32, (8, LANES), 0)
@@ -163,6 +161,9 @@
         return 0
 
     lax.fori_loop(1, n_b, send_ids, 0)
+    down_copy.start()
+    up_copy.start()
+    lax.fori_loop(first + 1, 2 * n_t - 1, load_w, 0)
 
     def msg(d, c):
         left = (d < i).astype(jnp.int32)
@@ -212,8 +213,6 @@
 
         return 0
 
-    first = 2 * (n_t - 1 - jnp.maximum(i, n_t - 1 - i)) + (i > n_t - 1 - i).astype(jnp.int32)
-
     def waits_x(s):
         return s == first
 
@@ -260,16 +259,31 @@
 
     lax.fori_loop(2, 2 * n_t - 1, project, 0)
 
-    def relay(d, left):
-        def chunk(c, _):
-            arrival(left, d, c).wait_recv()
-            part[d, rows_of(c)] = (
-                part[d, rows_of(c)].astype(F32) + rcv[left, d, rows_of(c)].astype(F32)
-            ).astype(BF16)
-            msg(d, c).start()
-            return 0
-
-        return chunk
+    near = (2 * i > n_t - 1).astype(jnp.int32)
+    inside = ((i > 0) & (i < n_t - 1)).astype(jnp.int32)
+    near_total = inside * chunks * jnp.maximum(i, n_t - 1 - i)
+    far_total = inside * chunks * jnp.minimum(i, n_t - 1 - i)
+
+    def relay(left, u):
+        b = u // chunks
+        c = u - b * chunks
+        d = left * b + (1 - left) * (n_t - 1 - b)
+        arrival(left, d, c).wait_recv()
+        part[d, rows_of(c)] = (
+            part[d, rows_of(c)].astype(F32) + rcv[left, d, rows_of(c)].astype(F32)
+        ).astype(BF16)
+        msg(d, c).start()
+
+    def relays(u, _):
+        @pl.when(u < near_total)
+        def _():
+            relay(near, u)
+
+        @pl.when((u >= 1) & (u <= far_total))
+        def _():
+            relay(1 - near, u - 1)
+
+        return 0
 
     def own_start(d):
         def chunk(c, _):
@@ -278,25 +292,8 @@
 
         return chunk
 
-    def relays(j, _):
-        def chunk(c, _):
-            right = n_t - 1 - j
-
-            @pl.when((right > i) & (i > 0))
-            def _():
-                relay(right, 0)(c, 0)
-
-            @pl.when((j < i) & (i < n_t - 1))
-            def _():
-                relay(j, 1)(c, 0)
-
-            return 0
-
-        return lax.fori_loop(0, chunks, chunk, 0)
-
-    @pl.when((i > 0) & (i < n_t - 1))
-    def _():
-        lax.fori_loop(0, n_t - 1, relays, 0)
+    split = jnp.maximum(near_total - 1, 0)
+    lax.fori_loop(0, split, relays, 0)
 
     def adapters_in(k, _):
         d = lax.rem(me + k, n_b)
@@ -378,30 +375,26 @@
     def _():
         lax.fori_loop(0, chunks, own_start(n_t - 2), 0)
 
+    lax.fori_loop(split, near_total + 1, relays, 0)
     dup[pl.ds(0, half), :] = own[...]
 
-    @pl.when(i > 0)
-    def _():
-        inner_in(0).wait_recv()
-        before = rin[0].astype(F32)
-        dup[pl.ds(0, half), :] += before
-
-        @pl.when(i < n_t - 1)
-        def _():
-            sin[0] = (own[...] + before).astype(BF16)
-            inner_msg(0).start()
-
-    @pl.when(i < n_t - 1)
-    def _():
-        inner_in(1).wait_recv()
-        after = rin[1].astype(F32)
-        dup[pl.ds(0, half), :] += after
-
-        @pl.when(i > 0)
-        def _():
-            sin[1] = (own[...] + after).astype(BF16)
-            inner_msg(1).start()
-
+    def exchange(k, _):
+        left = near + k - 2 * near * k
+
+        @pl.when(((left == 0) & (i > 0)) | ((left == 1) & (i < n_t - 1)))
+        def _():
+            inner_in(left).wait_recv()
+            came = rin[left].astype(F32)
+            dup[pl.ds(0, half), :] += came
+
+            @pl.when(inside == 1)
+            def _():
+                sin[left] = (own[...] + came).astype(BF16)
+                inner_msg(left).start()
+
+        return 0
+
+    lax.fori_loop(0, 2, exchange, 0)
     total = dup[pl.ds(0, half), :].astype(BF16).astype(F32)
     turned = pltpu.roll(total, rank, 1)
     dup[pl.ds(0, half), :] = jnp.where(low_lane, total, turned)

time: 88.2 us -> 66.6 us (0.76)
  Pallas kernels: 83.8 us -> 62.2 us
    pallas_call x1, Pallas kernels: 83.8 us -> 62.2 us  [shards(): pl.pallas_call(functools.partial(kernel, n_t, n_b, step), out_shape=(out,...]
where the time goes in v2:
time: 66.6 us; the launch traced here: 66.4 us
  Pallas kernels  62.2 us (93%)
  local copies, waits for them, and re-layouts  3.53 us (5%)
    pallas_call x1, Pallas kernels, shards(): pl.pallas_call(functools.partial(kernel, n_t, n_b, step), out_shape=(out,...  62.2 us
    unnamed x2, local copies, waits for them, and re-layouts  3.53 us

profile of v2, /device:TPU:0, one launch (start us, length us, event | category | flops | bytes accessed | tf_op | source)
XLA Modules:
  0.0 66.4 jit_solution(17394873689043577377)
XLA Ops:
  0.6 62.2 %shard_map.86 = (bf16[768,256]{1,0:T(8,128)(2,1)}, bf16[768,256]{1,0:T(8,128)(2,1)}) custom-call(s32[48]{0:T(128)} %ids.1, s32[128]{0:T(128)} %table.1, bf16[768,2048]{1,0:T(8,128)(2,1)} %normed_h.1, bf16[2048,1024]{1,0:T(8,128)(2,1)} %kw_h.1, bf16[2048,1024]{1,0:T(8,128)(2,1)} %vw_h.1, bf16[32,64,2048]{2,1,0:T(8,128)(2,1)} %down_h.1, bf16[32,64,256]{2,1,0:T(8,128)(2,1)} %up_h.1), custom_call_target="tpu_custom_call" | custom-call | flops 6442450944 | bytes 19922944 | tf_op jit(solution)/shard_map/pallas_call | solution.py:493
  62.9 1.8 %copy.11 = bf16[768,256]{1,0:T(8,128)(2,1)} copy(bf16[768,256]{1,0:T(8,128)(2,1)} %get-tuple-element.4) | data formatting | bytes 786432
  64.7 1.8 %copy.12 = bf16[768,256]{1,0:T(8,128)(2,1)} copy(bf16[768,256]{1,0:T(8,128)(2,1)} %get-tuple-element.5) | data formatting | bytes 786432

commit v3 on v2

--- a/solution.py
+++ b/solution.py
@@ -469,6 +469,11 @@
         inner_msg(1).wait_send()
 
 
+def hand_over(keys_i, vals_i, keys_o, vals_o):
+    keys_o[...] = keys_i[...]
+    vals_o[...] = vals_i[...]
+
+
 def shards(
     n_t,
     n_b,
@@ -483,14 +488,14 @@
     tokens, feats = normed.shape
     slots, rank, cols = adapter_up_factor.shape
     turns = turn_persona_ids.shape[0]
-    step = 256
+    step = tokens // 2
     chunks = tokens // step
     dma = pltpu.SemaphoreType.DMA
     any_space = pl.BlockSpec(memory_space=pl.ANY)
     smem = pl.BlockSpec(memory_space=pltpu.SMEM)
     vmem = pl.BlockSpec(memory_space=pltpu.VMEM)
     out = jax.ShapeDtypeStruct((tokens, cols), BF16)
-    return pl.pallas_call(
+    both = pl.pallas_call(
         functools.partial(kernel, n_t, n_b, step),
         out_shape=(out, out),
         in_specs=[smem, smem] + [any_space] * 5,
@@ -545,6 +550,12 @@
         adapter_down_factor,
         adapter_up_factor,
     )
+    return pl.pallas_call(
+        hand_over,
+        out_shape=(out, out),
+        in_specs=[vmem, vmem],
+        out_specs=(vmem, vmem),
+    )(*both)
 
 
 def solution(mesh):

time: 66.6 us -> 64.1 us (0.962)
  local copies, waits for them, and re-layouts: 3.53 us -> 0 us
  Pallas kernels: 62.2 us -> 63.3 us
    unnamed x2 -> x0, local copies, waits for them, and re-layouts: 3.53 us -> none
    pallas_call x0 -> x1, Pallas kernels: none -> 2.02 us  [shards(): pl.pallas_call(hand_over, out_shape=(out, out), in_specs=[vmem, vmem], ou...]
    pallas_call x1, Pallas kernels: 62.2 us -> 61.3 us  [shards(): pl.pallas_call(functools.partial(kernel, n_t, n_b, step), out_shape=(out,...]
where the time goes in v3:
time: 64.1 us; the launch traced here: 64 us
  Pallas kernels  63.3 us (99%)
    pallas_call x1, Pallas kernels, shards(): pl.pallas_call(functools.partial(kernel, n_t, n_b, step), out_shape=(out,...  61.3 us
    pallas_call x1, Pallas kernels, shards(): pl.pallas_call(hand_over, out_shape=(out, out), in_specs=[vmem, vmem], ou...  2.02 us

profile of v3, /device:TPU:0, one launch (start us, length us, event | category | flops | bytes accessed | tf_op | source)
XLA Modules:
  0.0 64.0 jit_solution(8528480479692222628)
XLA Ops:
  0.6 61.3 %shard_map.86 = (bf16[768,256]{1,0:T(8,128)(2,1)}, bf16[768,256]{1,0:T(8,128)(2,1)}) custom-call(s32[48]{0:T(128)} %ids.1, s32[128]{0:T(128)} %table.1, bf16[768,2048]{1,0:T(8,128)(2,1)} %normed_h.1, bf16[2048,1024]{1,0:T(8,128)(2,1)} %kw_h.1, bf16[2048,1024]{1,0:T(8,128)(2,1)} %vw_h.1, bf16[32,64,2048]{2,1,0:T(8,128)(2,1)} %down_h.1, bf16[32,64,256]{2,1,0:T(8,128)(2,1)} %up_h.1), custom_call_target="tpu_custom_call" | custom-call | flops 6442450944 | bytes 19922944 | tf_op jit(solution)/shard_map/pallas_call | solution.py:498
  61.9 2.0 %shard_map.87 = (bf16[768,256]{1,0:T(8,128)(2,1)}, bf16[768,256]{1,0:T(8,128)(2,1)}) custom-call(bf16[768,256]{1,0:T(8,128)(2,1)} %get-tuple-element.4.keys_i, bf16[768,256]{1,0:T(8,128)(2,1)} %get-tuple-element.5.vals_i), custom_call_target="tpu_custom_call" | custom-call | tf_op jit(solution)/shard_map/pallas_call | solution.py:553
